TPU v7x, 32 devices: a whole 2x2x4 slice. The times are simulated.
32 devices in a mesh: face: 2 (over core), sub: 16 (over z, y, x).
Axes of the slice: x: 2, y: 2, z: 4, core: 2. Of those that a mesh axis runs over, the one named last changes fastest.
Arguments:
- features: bfloat16 [768, 24, 192], P(('face', 'sub')), may hold values from -6 to 6
- w_first: bfloat16 [3, 3, 192, 192], replicated, may hold values from -0.15625 to 0.15625
- b_first: float32 [192], replicated, may hold values from -3 to 3
- w_second: bfloat16 [3, 3, 192, 192], replicated, may hold values from -0.15625 to 0.15625
- neighbours: int32 [32, 4], replicated, may hold values from 0 to 31, as said below
- rotations: int32 [32, 4], replicated, may hold values from 0 to 3
- cotangent: bfloat16 [384, 12, 192], P(('face', 'sub')), may hold values from -6 to 6
Outputs:
- pooled: bfloat16 [384, 12, 192], P(('face', 'sub'))
- grad_input: bfloat16 [768, 24, 192], P(('face', 'sub'))
- grad_w1: float32 [3, 3, 192, 192], replicated
- grad_b1: float32 [192], replicated
- grad_w2: float32 [3, 3, 192, 192], replicated
Inputs may be any that keep to these rules, and one draw needn't show every extreme that they name: neighbours[d, e] is a tile f * 16 + s other than d; it has the same f as d or the same s as d; two tiles of the same f share at most one edge, and no tile names the same tile of its own f at two edges.
All inputs are finite; a program needn't handle non-finite values.
Results may differ from a plain program's by a relative error of at most 0.012.
Values may be sent and summed in bfloat16 or wider, within the bound.
A program may use at most 64 MiB of HBM per device.

v0:
```python
import math

import jax
import jax.numpy as jnp
import numpy as np
from jax import lax
from jax.sharding import PartitionSpec as P


def rim_lookup():
    return np.array(
        [
            [[0, 0], [1, 0], [2, 0], [3, 0]],
            [[1, 0], [2, 1], [3, 0], [0, 1]],
            [[2, 1], [3, 1], [0, 1], [1, 1]],
            [[3, 1], [0, 0], [1, 1], [2, 0]],
        ],
        np.int32,
    )


def edge_codes(rotations):
    lookup = rim_lookup()[:, [2, 3, 0, 1], :]
    quarters = rotations[:, :, None] == jnp.arange(4, dtype=jnp.int32)[None, None, :]
    anchor_tab = jnp.asarray(lookup[:, :, 0].T)
    flip_tab = jnp.asarray(lookup[:, :, 1].T)
    anchors = jnp.sum(jnp.where(quarters, anchor_tab[None], 0), axis=2).astype(jnp.int32)
    flip_codes = jnp.sum(jnp.where(quarters, flip_tab[None], 0), axis=2).astype(jnp.int32)
    return (anchors, flip_codes)


def layout(neighbours, rotations):
    sub_count = lax.axis_size("sub")
    face_count = lax.axis_size("face")
    face_id = lax.axis_index("face")
    sub_id = lax.axis_index("sub")
    device = face_id * sub_count + sub_id
    anchors, flip_codes = edge_codes(rotations)

    def by_face(table_in):
        return lax.dynamic_index_in_dim(
            table_in.reshape(face_count, sub_count, 4), sub_id, 1, keepdims=False
        )

    def by_block(table_in):
        return lax.dynamic_slice_in_dim(table_in, face_id * sub_count, sub_count, 0)

    return {
        "device": device,
        "face_id": face_id,
        "sub_count": sub_count,
        "mine_nbr": lax.dynamic_index_in_dim(neighbours, device, 0, keepdims=False),
        "mine_anchor": lax.dynamic_index_in_dim(anchors, device, 0, keepdims=False),
        "mine_flip": lax.dynamic_index_in_dim(flip_codes, device, 0, keepdims=False),
        "block_nbr": by_block(neighbours),
        "block_anchor": by_block(anchors),
        "block_flip": by_block(flip_codes),
        "cross_nbr": by_face(neighbours),
        "cross_anchor": by_face(anchors),
    }


def outer_rows(square):
    return jnp.stack([square[0], square[:, -1], square[-1], square[:, 0]], axis=0)


def border_rows(padded):
    return jnp.stack([padded[0, 1:-1], padded[1:-1, -1], padded[-1, 1:-1], padded[1:-1, 0]], axis=0)


def flip_where(rows_in, flag_vec):
    return jnp.where(flag_vec[:, None, None] == 1, rows_in[:, ::-1], rows_in)


def surround(square, picked):
    padded = jnp.pad(square, ((1, 1), (1, 1), (0, 0)))
    padded = padded.at[0, 1:-1].set(picked[0])
    padded = padded.at[1:-1, -1].set(picked[1])
    padded = padded.at[-1, 1:-1].set(picked[2])
    padded = padded.at[1:-1, 0].set(picked[3])
    return padded


def fetch_halo(square, layout_info):
    extent, channels = (square.shape[0], square.shape[2])
    sub_count = layout_info["sub_count"]
    mine_nbr = layout_info["mine_nbr"]
    mine_anchor = layout_info["mine_anchor"]
    mine_flip = layout_info["mine_flip"]
    same_face = mine_nbr // sub_count == layout_info["face_id"]
    own_rows = outer_rows(square)
    from_face = lax.all_gather(own_rows[None], "face", axis=0, tiled=True).reshape(
        -1, extent * channels
    )
    face_slots = mine_nbr // sub_count * 4 + mine_anchor
    face_pick = (
        face_slots[:, None] == jnp.arange(from_face.shape[0], dtype=jnp.int32)[None, :]
    ) & jnp.logical_not(same_face)[:, None]
    across = jnp.dot(face_pick.astype(jnp.bfloat16), from_face, preferred_element_type=jnp.float32)
    from_block = lax.all_gather(own_rows[None], "sub", axis=0, tiled=True).reshape(
        -1, extent * channels
    )
    block_slots = mine_nbr % sub_count * 4 + mine_anchor
    block_pick = (
        block_slots[:, None] == jnp.arange(from_block.shape[0], dtype=jnp.int32)[None, :]
    ) & same_face[:, None]
    inside = jnp.dot(
        block_pick.astype(jnp.bfloat16), from_block, preferred_element_type=jnp.float32
    )
    picked = flip_where(
        (inside + across).astype(jnp.bfloat16).reshape(4, extent, channels), mine_flip
    )
    return picked


def return_halo(summed, layout_info):
    extent, channels = (summed.shape[0] - 2, summed.shape[2])
    device = layout_info["device"]
    border_ids = jnp.arange(4, dtype=jnp.int32)[None, None, :]
    own_rows = flip_where(border_rows(summed), layout_info["mine_flip"])
    from_face = (
        lax.all_gather(own_rows[None].astype(jnp.bfloat16), "face", axis=0, tiled=True)
        .astype(jnp.float32)
        .reshape(-1, extent * channels)
    )
    cross_mask = (layout_info["cross_nbr"] == device)[:, :, None] & (
        layout_info["cross_anchor"][:, :, None] == border_ids
    )
    arrived = lax.dot_general(
        cross_mask.reshape(-1, 4).astype(jnp.float32),
        from_face,
        (((0,), (0,)), ((), ())),
        precision=lax.Precision.HIGHEST,
        preferred_element_type=jnp.float32,
    )
    block_hits = (layout_info["block_nbr"] == device)[:, :, None] & (
        layout_info["block_anchor"][:, :, None] == border_ids
    )
    from_block = (
        lax.all_gather(own_rows[None].astype(jnp.bfloat16), "sub", axis=0, tiled=True)
        .astype(jnp.float32)
        .reshape(-1, extent * channels)
    )
    block_mask = block_hits.reshape(-1, 4).astype(jnp.float32)
    arrived = arrived + lax.dot_general(
        block_mask,
        from_block,
        (((0,), (0,)), ((), ())),
        precision=lax.Precision.HIGHEST,
        preferred_element_type=jnp.float32,
    )
    arrived = arrived.reshape(4, extent, channels)
    middle = summed[1:-1, 1:-1]
    middle = middle.at[0].add(arrived[0])
    middle = middle.at[:, -1].add(arrived[1])
    middle = middle.at[-1].add(arrived[2])
    middle = middle.at[:, 0].add(arrived[3])
    return middle


def gather_windows(padded, extent):
    portions = []
    for row_off in range(3):
        for col_off in range(3):
            portions.append(
                padded[row_off : row_off + extent, col_off : col_off + extent].reshape(
                    extent * extent, -1
                )
            )
    return jnp.concatenate(portions, axis=1)


def scatter_windows(spread, extent, channels):
    summed = jnp.zeros((extent + 2, extent + 2, channels), jnp.float32)
    for row_off in range(3):
        for col_off in range(3):
            offset_id = 3 * row_off + col_off
            portion = spread[:, offset_id * channels : (offset_id + 1) * channels].reshape(
                extent, extent, channels
            )
            summed = summed.at[row_off : row_off + extent, col_off : col_off + extent].add(portion)
    return summed


def local(features, w_first, b_first, w_second, neighbours, rotations, cotangent):
    extent, channels = (features.shape[1], features.shape[2])
    half_side = extent // 2
    layout_info = layout(neighbours, rotations)
    first_flat = w_first.reshape(9 * channels, channels)
    second_flat = w_second.reshape(9 * channels, channels)
    padded_in = surround(features, fetch_halo(features, layout_info))
    windows_in = gather_windows(padded_in, extent)
    hidden = jnp.dot(windows_in, first_flat, preferred_element_type=jnp.float32) + b_first
    active = jax.nn.silu(hidden).astype(jnp.bfloat16).reshape(extent, extent, channels)
    padded_act = surround(active, fetch_halo(active, layout_info))
    windows_act = gather_windows(padded_act, extent)
    second = jnp.dot(windows_act, second_flat, preferred_element_type=jnp.float32)
    summed_out = features.reshape(extent * extent, channels).astype(jnp.float32) + second
    pooled = (
        summed_out.reshape(half_side, 2, half_side, 2, channels)
        .mean(axis=(1, 3))
        .astype(jnp.bfloat16)
    )
    upward = (cotangent.astype(jnp.float32) * 0.25).astype(jnp.bfloat16)
    grad_out = jnp.broadcast_to(upward[:, None, :, None, :], (half_side, 2, half_side, 2, channels))
    grad_out = grad_out.reshape(extent * extent, channels)
    contract_rows = (((0,), (0,)), ((), ()))
    contract_cols = (((1,), (1,)), ((), ()))
    sum_w2 = lax.dot_general(
        windows_act, grad_out, contract_rows, preferred_element_type=jnp.float32
    )
    spread_two = lax.dot_general(
        grad_out, second_flat, contract_cols, preferred_element_type=jnp.float32
    )
    grad_active = return_halo(scatter_windows(spread_two, extent, channels), layout_info).astype(
        jnp.bfloat16
    )
    sigmoid_h = jax.nn.sigmoid(hidden)
    grad_hidden = (
        grad_active.reshape(extent * extent, channels).astype(jnp.float32)
        * sigmoid_h
        * (1.0 + hidden * (1.0 - sigmoid_h))
    )
    grad_hidden = grad_hidden.astype(jnp.bfloat16)
    sum_b1 = jnp.sum(grad_hidden, axis=0, dtype=jnp.float32)
    sum_w1 = lax.dot_general(
        windows_in, grad_hidden, contract_rows, preferred_element_type=jnp.float32
    )
    spread_one = lax.dot_general(
        grad_hidden, first_flat, contract_cols, preferred_element_type=jnp.float32
    )
    grad_input = return_halo(scatter_windows(spread_one, extent, channels), layout_info)
    grad_input = (
        grad_input + grad_out.astype(jnp.float32).reshape(extent, extent, channels)
    ).astype(jnp.bfloat16)
    total_w1, total_b1, total_w2 = lax.psum((sum_w1, sum_b1, sum_w2), ("face", "sub"))
    grad_scale = 1.0 / math.sqrt(neighbours.shape[0] * extent * extent)
    return (
        pooled,
        grad_input,
        (total_w1 * grad_scale).reshape(3, 3, channels, channels),
        total_b1 * grad_scale,
        (total_w2 * grad_scale).reshape(3, 3, channels, channels),
    )


def solution(mesh):
    in_specs = (
        P(("face", "sub"), None, None),
        P(),
        P(),
        P(),
        P(),
        P(),
        P(("face", "sub"), None, None),
    )
    out_specs = (P(("face", "sub"), None, None), P(("face", "sub"), None, None), P(), P(), P())
    return jax.shard_map(local, mesh=mesh, in_specs=in_specs, out_specs=out_specs, check_vma=False)
```

profile of v0, /device:TPU:1, one launch (start us, length us, event | category | flops | bytes accessed | tf_op | source)
XLA Modules:
  0.0 458.6 jit_solution(812224152784849294)
XLA Ops:
  17.3 6.1 %scatter-add.89 = f32[26,26,192]{2,0,1:T(8,128)S(1)} dynamic-update-slice(f32[26,26,192]{2,0,1:T(8,128)S(1)} %scatter-add.86, f32[24,24,192]{2,0,1:T(8,128)S(1)} %copy_add_fusion.2, s32[]{:T(128)} %bitcast.3, s32[]{:T(128)} %bitcast.4, s32[]{:T(128)} %constant.897.clone.1) | dynamic-update-slice | bytes 884740 | tf_op jit(solution)/shard_map/scatter-add | solution.py:181
  23.4 3.1 add_select_fusion.1
  26.5 6.0 %scatter-add.90 = f32[26,26,192]{2,0,1:T(8,128)S(1)} dynamic-update-slice(f32[26,26,192]{2,0,1:T(8,128)S(1)} %scatter-add.89, f32[24,24,192]{2,0,1:T(8,128)S(1)} %add_select_fusion.1, s32[]{:T(128)} %bitcast.34, s32[]{:T(128)} %bitcast.35, s32[]{:T(128)} %constant.897.clone.1) | dynamic-update-slice | bytes 884740 | tf_op jit(solution)/shard_map/scatter-add | solution.py:181
  33.8 5.1 %scatter-add.91 = f32[26,26,192]{2,0,1:T(8,128)S(1)} dynamic-update-slice(f32[26,26,192]{2,0,1:T(8,128)S(1)} %scatter-add.90, f32[24,24,192]{2,0,1:T(8,128)S(1)} %slice_add_fusion.11, s32[]{:T(128)} %constant.903.clone.1, s32[]{:T(128)} %constant.897.clone.1, s32[]{:T(128)} %constant.897.clone.1) | dynamic-update-slice | bytes 884740 | tf_op jit(solution)/shard_map/scatter-add | solution.py:181
  40.2 4.9 %scatter-add.94 = f32[26,26,192]{2,0,1:T(8,128)S(1)} dynamic-update-slice(f32[26,26,192]{2,0,1:T(8,128)S(1)} %scatter-add.91, f32[24,24,192]{2,0,1:T(8,128)S(1)} %slice_add_fusion.10, s32[]{:T(128)} %constant.903.clone.1, s32[]{:T(128)} %constant.903.clone.1, s32[]{:T(128)} %constant.897.clone.1) | dynamic-update-slice | bytes 884740 | tf_op jit(solution)/shard_map/scatter-add | solution.py:181
  46.4 4.8 %scatter-add.95 = f32[26,26,192]{2,0,1:T(8,128)S(1)} dynamic-update-slice(f32[26,26,192]{2,0,1:T(8,128)S(1)} %scatter-add.94, f32[24,24,192]{2,0,1:T(8,128)S(1)} %slice_add_fusion.9, s32[]{:T(128)} %constant.903.clone.1, s32[]{:T(128)} %constant.911.clone.1, s32[]{:T(128)} %constant.897.clone.1) | dynamic-update-slice | bytes 884740 | tf_op jit(solution)/shard_map/scatter-add | solution.py:181
  52.5 5.1 %scatter-add.96 = f32[26,26,192]{2,0,1:T(8,128)S(1)} dynamic-update-slice(f32[26,26,192]{2,0,1:T(8,128)S(1)} %scatter-add.95, f32[24,24,192]{2,0,1:T(8,128)S(1)} %slice_add_fusion.8, s32[]{:T(128)} %constant.911.clone.1, s32[]{:T(128)} %constant.897.clone.1, s32[]{:T(128)} %constant.897.clone.1) | dynamic-update-slice | bytes 884740 | tf_op jit(solution)/shard_map/scatter-add | solution.py:181
  58.9 4.9 %scatter-add.99 = f32[26,26,192]{2,0,1:T(8,128)S(1)} dynamic-update-slice(f32[26,26,192]{2,0,1:T(8,128)S(1)} %scatter-add.96, f32[24,24,192]{2,0,1:T(8,128)S(1)} %slice_add_fusion.7, s32[]{:T(128)} %constant.911.clone.1, s32[]{:T(128)} %constant.903.clone.1, s32[]{:T(128)} %constant.897.clone.1) | dynamic-update-slice | bytes 884740 | tf_op jit(solution)/shard_map/scatter-add | solution.py:181
  64.1 4.8 %scatter-add.100 = f32[26,26,192]{2,0,1:T(8,128)S(1)} dynamic-update-slice(f32[26,26,192]{2,0,1:T(8,128)S(1)} %scatter-add.99, f32[24,24,192]{2,0,1:T(8,128)S(1)} %slice_add_fusion.6, s32[]{:T(128)} %constant.911.clone.1, s32[]{:T(128)} %constant.911.clone.1, s32[]{:T(128)} %constant.897.clone.1) | dynamic-update-slice | bytes 884740 | tf_op jit(solution)/shard_map/scatter-add | solution.py:181
  70.8 39.8 %all-gather = bf16[64,24,192]{2,1,0:T(8,128)(2,1)S(1)} all-gather(bf16[4,24,192]{2,1,0:T(8,128)(2,1)S(1)} %pad_maximum_fusion.2), channel_id=2, replica_groups=mesh['face'=2,'sub'=16] {'sub'}, dimensions={0}, use_global_device_ids=true | all-gather | bytes 626688 | tf_op jit(solution)/shard_map/all_gather | solution.py:100
  110.5 8.8 %all-gather.1 = bf16[8,24,192]{2,1,0:T(8,128)(2,1)S(1)} all-gather(bf16[4,24,192]{2,1,0:T(8,128)(2,1)S(1)} %pad_maximum_fusion.2), channel_id=3, replica_groups=mesh['face'=2,'sub'=16] {'face'}, dimensions={0}, use_global_device_ids=true | all-gather | bytes 110592 | tf_op jit(solution)/shard_map/all_gather | solution.py:92
  127.4 33.6 %all-gather.5 = bf16[64,24,192]{2,1,0:T(8,128)(2,1)S(1)} all-gather(bf16[4,24,192]{2,1,0:T(8,128)(2,1)S(1)} %get-tuple-element.535), channel_id=7, replica_groups=mesh['face'=2,'sub'=16] {'sub'}, dimensions={0}, use_global_device_ids=true | all-gather | bytes 626688 | tf_op jit(solution)/shard_map/all_gather | solution.py:140
  161.0 8.0 %all-gather.4 = bf16[8,24,192]{2,1,0:T(8,128)(2,1)S(1)} all-gather(bf16[4,24,192]{2,1,0:T(8,128)(2,1)S(1)} %get-tuple-element.535), channel_id=6, replica_groups=mesh['face'=2,'sub'=16] {'face'}, dimensions={0}, use_global_device_ids=true | all-gather | bytes 110592 | tf_op jit(solution)/shard_map/all_gather | solution.py:122
  181.6 3.8 concatenate.84
  185.4 3.4 convert_reduce_fusion
  196.5 38.3 %all-gather.2 = bf16[64,24,192]{2,1,0:T(8,128)(2,1)} all-gather(bf16[4,24,192]{2,1,0:T(8,128)(2,1)S(1)} %pad_maximum_fusion.3), channel_id=4, replica_groups=mesh['face'=2,'sub'=16] {'sub'}, dimensions={0}, use_global_device_ids=true | all-gather | bytes 626688 | tf_op jit(solution)/shard_map/all_gather | solution.py:100
  234.8 8.5 %all-gather.3 = bf16[8,24,192]{2,1,0:T(8,128)(2,1)} all-gather(bf16[4,24,192]{2,1,0:T(8,128)(2,1)S(1)} %pad_maximum_fusion.3), channel_id=5, replica_groups=mesh['face'=2,'sub'=16] {'face'}, dimensions={0}, use_global_device_ids=true | all-gather | bytes 110592 | tf_op jit(solution)/shard_map/all_gather | solution.py:92
  249.7 6.1 %scatter-add.110 = f32[26,26,192]{2,0,1:T(8,128)S(1)} dynamic-update-slice(f32[26,26,192]{2,0,1:T(8,128)S(1)} %scatter-add.109, f32[24,24,192]{2,0,1:T(8,128)S(1)} %copy_add_fusion.1, s32[]{:T(128)} %bitcast.3, s32[]{:T(128)} %bitcast.4, s32[]{:T(128)} %constant.897.clone.1) | dynamic-update-slice | bytes 884740 | tf_op jit(solution)/shard_map/scatter-add | solution.py:181
  255.8 3.1 add_select_fusion
  258.9 6.0 %scatter-add.111 = f32[26,26,192]{2,0,1:T(8,128)S(1)} dynamic-update-slice(f32[26,26,192]{2,0,1:T(8,128)S(1)} %scatter-add.110, f32[24,24,192]{2,0,1:T(8,128)S(1)} %add_select_fusion, s32[]{:T(128)} %bitcast.34, s32[]{:T(128)} %bitcast.35, s32[]{:T(128)} %constant.897.clone.1) | dynamic-update-slice | bytes 884740 | tf_op jit(solution)/shard_map/scatter-add | solution.py:181
  266.2 5.1 %scatter-add.114 = f32[26,26,192]{2,0,1:T(8,128)S(1)} dynamic-update-slice(f32[26,26,192]{2,0,1:T(8,128)S(1)} %scatter-add.111, f32[24,24,192]{2,0,1:T(8,128)S(1)} %slice_add_fusion.5, s32[]{:T(128)} %constant.903.clone.1, s32[]{:T(128)} %constant.897.clone.1, s32[]{:T(128)} %constant.897.clone.1) | dynamic-update-slice | bytes 884740 | tf_op jit(solution)/shard_map/scatter-add | solution.py:181
  272.6 4.9 %scatter-add.115 = f32[26,26,192]{2,0,1:T(8,128)S(1)} dynamic-update-slice(f32[26,26,192]{2,0,1:T(8,128)S(1)} %scatter-add.114, f32[24,24,192]{2,0,1:T(8,128)S(1)} %slice_add_fusion.4, s32[]{:T(128)} %constant.903.clone.1, s32[]{:T(128)} %constant.903.clone.1, s32[]{:T(128)} %constant.897.clone.1) | dynamic-update-slice | bytes 884740 | tf_op jit(solution)/shard_map/scatter-add | solution.py:181
  277.8 4.8 %scatter-add.116 = f32[26,26,192]{2,0,1:T(8,128)S(1)} dynamic-update-slice(f32[26,26,192]{2,0,1:T(8,128)S(1)} %scatter-add.115, f32[24,24,192]{2,0,1:T(8,128)S(1)} %slice_add_fusion.3, s32[]{:T(128)} %constant.903.clone.1, s32[]{:T(128)} %constant.911.clone.1, s32[]{:T(128)} %constant.897.clone.1) | dynamic-update-slice | bytes 884740 | tf_op jit(solution)/shard_map/scatter-add | solution.py:181
  282.8 5.1 %scatter-add.119 = f32[26,26,192]{2,0,1:T(8,128)S(1)} dynamic-update-slice(f32[26,26,192]{2,0,1:T(8,128)S(1)} %scatter-add.116, f32[24,24,192]{2,0,1:T(8,128)S(1)} %slice_add_fusion.2, s32[]{:T(128)} %constant.911.clone.1, s32[]{:T(128)} %constant.897.clone.1, s32[]{:T(128)} %constant.897.clone.1) | dynamic-update-slice | bytes 884740 | tf_op jit(solution)/shard_map/scatter-add | solution.py:181
  288.1 4.9 %scatter-add.120 = f32[26,26,192]{2,0,1:T(8,128)S(1)} dynamic-update-slice(f32[26,26,192]{2,0,1:T(8,128)S(1)} %scatter-add.119, f32[24,24,192]{2,0,1:T(8,128)S(1)} %slice_add_fusion.1, s32[]{:T(128)} %constant.911.clone.1, s32[]{:T(128)} %constant.903.clone.1, s32[]{:T(128)} %constant.897.clone.1) | dynamic-update-slice | bytes 884740 | tf_op jit(solution)/shard_map/scatter-add | solution.py:181
  294.5 4.8 %scatter-add.121 = f32[26,26,192]{2,0,1:T(8,128)S(1)} dynamic-update-slice(f32[26,26,192]{2,0,1:T(8,128)S(1)} %scatter-add.120, f32[24,24,192]{2,0,1:T(8,128)S(1)} %slice_add_fusion, s32[]{:T(128)} %constant.911.clone.1, s32[]{:T(128)} %constant.911.clone.1, s32[]{:T(128)} %constant.897.clone.1) | dynamic-update-slice | bytes 884740 | tf_op jit(solution)/shard_map/scatter-add | solution.py:181
  305.8 3.8 concatenate.85
  312.2 40.5 %all-gather.7 = bf16[64,24,192]{2,1,0:T(8,128)(2,1)} all-gather(bf16[4,24,192]{2,1,0:T(8,128)(2,1)S(1)} %copy-done.9), channel_id=9, replica_groups=mesh['face'=2,'sub'=16] {'sub'}, dimensions={0}, use_global_device_ids=true | all-gather | bytes 626688 | tf_op jit(solution)/shard_map/all_gather | solution.py:140
  352.7 7.4 %all-gather.6 = bf16[8,24,192]{2,1,0:T(8,128)(2,1)S(1)} all-gather(bf16[4,24,192]{2,1,0:T(8,128)(2,1)S(1)} %copy-done.9), channel_id=8, replica_groups=mesh['face'=2,'sub'=16] {'face'}, dimensions={0}, use_global_device_ids=true | all-gather | bytes 110592 | tf_op jit(solution)/shard_map/all_gather | solution.py:122
  379.6 2.7 convolution_add_fusion.4
  384.4 36.3 %psum.22 = f32[192]{0:T(256)S(1)} all-reduce(f32[192]{0:T(256)S(1)} %copy-done.34), channel_id=1, replica_groups=mesh['face'=2,'sub'=16] {'face','sub'}, use_global_device_ids=true, to_apply=%region_6.7 | all-reduce | flops 192 | bytes 1536 | tf_op jit(solution)/shard_map/psum | solution.py:236
  422.0 23.3 %all-reduce.7.cloned.1.call-done = (f32[1728,192]{0,1:T(8,128)}, f32[1728,192]{0,1:T(8,128)}) async-done(((f32[1728,192]{0,1:T(8,128)}, f32[1728,192]{0,1:T(8,128)}), (f32[1728,192]{0,1:T(8,128)}, f32[1728,192]{0,1:T(8,128)})) %all-reduce.7.cloned.1.call-update) | async-done | bytes 2654224 | tf_op jit(solution)/shard_map/psum | solution.py:236
  (239 shorter events, 95.9 us)
Async XLA Ops:
  7.2 178.2 %copy-start = (bf16[3,3,192,192]{3,2,1,0:T(8,128)(2,1)S(1)}, bf16[3,3,192,192]{3,2,1,0:T(8,128)(2,1)}, u32[]{:S(2)}) copy-start(bf16[3,3,192,192]{3,2,1,0:T(8,128)(2,1)} %param.78) | copy-start | bytes 1990660
  7.2 438.1 %all-reduce.7.cloned.1.call-start = ((), (), s32[]{:S(2)}) async-start(), calls=%async_computation | async-start | bytes 5505024 | tf_op jit(solution)/shard_map/psum | solution.py:236
  63.8 55.7 %copy-start.31 = (s32[32,4]{0,1:T(4,128)S(1)}, s32[32,4]{0,1:T(4,128)}, u32[]{:S(2)}) copy-start(s32[32,4]{0,1:T(4,128)} %param.82) | copy-start | bytes 1540
  63.8 55.7 %copy-start.32 = (s32[4,4]{1,0:T(4,128)S(1)}, s32[4,4]{1,0:T(4,128)}, u32[]{:S(2)}) copy-start(s32[4,4]{1,0:T(4,128)} %constant.917.clone) | copy-start | bytes 196
  63.9 55.7 %copy-start.33 = (s32[4,4]{1,0:T(4,128)S(1)}, s32[4,4]{1,0:T(4,128)}, u32[]{:S(2)}) copy-start(s32[4,4]{1,0:T(4,128)} %constant.918.clone) | copy-start | bytes 196
  63.9 56.4 %copy-start.17 = (s32[32,4]{0,1:T(4,128)S(1)}, s32[32,4]{0,1:T(4,128)}, u32[]{:S(2)}) copy-start(s32[32,4]{0,1:T(4,128)} %param.81) | copy-start | bytes 1540
  69.0 51.9 %copy-start.11 = (bf16[1,24,192]{2,1,0:T(8,128)(2,1)}, bf16[1,24,192]{2,1,0:T(8,128)(2,1)S(1)}, u32[]{:S(2)}) copy-start(bf16[1,24,192]{2,1,0:T(8,128)(2,1)S(1)} %get-tuple-element.494) | copy-start | bytes 27652
  69.0 51.9 %copy-start.12 = (bf16[1,24,192]{2,1,0:T(8,128)(2,1)}, bf16[1,24,192]{2,1,0:T(8,128)(2,1)S(1)}, u32[]{:S(2)}) copy-start(bf16[1,24,192]{2,1,0:T(8,128)(2,1)S(1)} %get-tuple-element.495) | copy-start | bytes 27652
  122.8 46.2 %copy-start.16 = (s32[32,4]{0,1:T(4,128)S(1)}, s32[32,4]{0,1:T(4,128)}, u32[]{:S(2)}) copy-start(s32[32,4]{0,1:T(4,128)} %copy-done.15) | copy-start | bytes 1540
  122.8 46.3 %copy-start.18 = (s32[32,4]{0,1:T(4,128)S(1)}, s32[32,4]{0,1:T(4,128)}, u32[]{:S(2)}) copy-start(s32[32,4]{0,1:T(4,128)} %param.81) | copy-start | bytes 1540
  123.7 3.7 copy-start.23
  123.7 3.7 copy-start.36
  126.5 43.7 %copy-start.19 = (pred[4]{0:T(512)(128)(4,1)}, pred[4]{0:T(512)(128)(4,1)S(1)}, u32[]{:S(2)}) copy-start(pred[4]{0:T(512)(128)(4,1)S(1)} %fusion.27) | copy-start | bytes 16
  175.1 4.8 %copy-start.4 = (f32[24,24,192]{2,0,1:T(8,128)S(1)}, f32[24,24,192]{2,0,1:T(8,128)}, u32[]{:S(2)}) copy-start(f32[24,24,192]{2,0,1:T(8,128)} %slice.1244) | copy-start | bytes 1327108
  177.0 2.2 copy-start.27
  179.4 2.1 copy-start.7
  181.6 3.8 copy-start.39
  288.1 11.2 %copy-start.6 = (bf16[576,192]{1,0:T(8,128)(2,1)S(1)}, bf16[576,192]{1,0:T(8,128)(2,1)}, u32[]{:S(2)}) copy-start(bf16[576,192]{1,0:T(8,128)(2,1)} %copy.330) | copy-start | bytes 663556
  293.1 6.4 %copy-start.3 = (bf16[64,24,192]{2,1,0:T(8,128)(2,1)S(1)}, bf16[64,24,192]{2,1,0:T(8,128)(2,1)}, u32[]{:S(2)}) copy-start(bf16[64,24,192]{2,1,0:T(8,128)(2,1)} %all-gather.2) | copy-start | bytes 1769476
  294.5 5.7 %copy-start.22 = (pred[4]{0:T(512)(128)(4,1)S(1)}, pred[4]{0:T(512)(128)(4,1)}, u32[]{:S(2)}) copy-start(pred[4]{0:T(512)(128)(4,1)} %get-tuple-element.468) | copy-start | bytes 16
  294.5 5.7 %copy-start.24 = (s32[4]{0:T(128)S(1)}, s32[4]{0:T(128)}, u32[]{:S(2)}) copy-start(s32[4]{0:T(128)} %copy-done.23) | copy-start | bytes 52
  294.5 6.0 %copy-start.10 = (bf16[8,24,192]{2,1,0:T(8,128)(2,1)S(1)}, bf16[8,24,192]{2,1,0:T(8,128)(2,1)}, u32[]{:S(2)}) copy-start(bf16[8,24,192]{2,1,0:T(8,128)(2,1)} %all-gather.3) | copy-start | bytes 221188
  294.5 6.1 %copy-start.35 = (pred[4]{0:T(512)(128)(4,1)S(1)}, pred[4]{0:T(512)(128)(4,1)}, u32[]{:S(2)}) copy-start(pred[4]{0:T(512)(128)(4,1)} %get-tuple-element.467) | copy-start | bytes 16
  294.5 6.1 %copy-start.37 = (s32[4]{0:T(128)S(1)}, s32[4]{0:T(128)}, u32[]{:S(2)}) copy-start(s32[4]{0:T(128)} %copy-done.36) | copy-start | bytes 52
  311.5 52.1 %copy-start.28 = (pred[8]{0:T(512)(128)(4,1)S(1)}, pred[8]{0:T(512)(128)(4,1)}, u32[]{:S(2)}) copy-start(pred[8]{0:T(512)(128)(4,1)} %copy-done.27) | copy-start | bytes 28
  311.5 52.1 %copy-start.30 = (s32[8]{0:T(128)S(1)}, s32[8]{0:T(128)}, u32[]{:S(2)}) copy-start(s32[8]{0:T(128)} %copy-done.29) | copy-start | bytes 100
  311.5 52.4 %copy-start.26 = (s32[64]{0:T(128)S(1)}, s32[64]{0:T(128)}, u32[]{:S(2)}) copy-start(s32[64]{0:T(128)} %copy-done.25) | copy-start | bytes 772
  360.1 12.9 %copy-start.8 = (f32[12,12,192]{2,1,0:T(8,128)S(1)}, f32[12,12,192]{2,1,0:T(8,128)}, u32[]{:S(2)}) copy-start(f32[12,12,192]{2,1,0:T(8,128)} %get-tuple-element.523) | copy-start | bytes 331780
  371.5 5.1 %copy-start.5 = (bf16[24,24,192]{2,1,0:T(8,128)(2,1)S(1)}, bf16[24,24,192]{2,1,0:T(8,128)(2,1)}, u32[]{:S(2)}) copy-start(bf16[24,24,192]{2,1,0:T(8,128)(2,1)} %param.77) | copy-start | bytes 663556
  374.4 5.2 %copy-start.2 = (bf16[3,3,192,192]{3,2,1,0:T(8,128)(2,1)S(1)}, bf16[3,3,192,192]{3,2,1,0:T(8,128)(2,1)}, u32[]{:S(2)}) copy-start(bf16[3,3,192,192]{3,2,1,0:T(8,128)(2,1)} %param.80) | copy-start | bytes 1990660
  382.3 2.1 copy-start.34
  448.5 3.3 copy-start.1
  (9 other events, 12.8 us)
Sparse Core Ops, SparseCore 0:
  311.6 133.6 all-reduce.6
where the time goes:
time: 463 us; the launch traced here: 459 us
  blocking collectives  221 us (48%)
  local copies, waits for them, and re-layouts  142 us (31%)
  other arithmetic  39.1 us (8%)
  waiting for transfers between devices  23.4 us (5%)
  matrix products  18 us (4%)
  between operations  15.1 us (3%)
    scatter-add x18, local copies, waits for them, and re-layouts, scatter_windows(): summed.at[row_off:row_off + extent, col_off:col_off + extent].add(portion)  83.3 us
    all_gather x2, blocking collectives, fetch_halo(): lax.all_gather(own_rows[None], 'sub', axis=0, tiled=True)  78.1 us
    all_gather x2, blocking collectives, return_halo(): lax.all_gather(own_rows[None].astype(jnp.bfloat16), 'sub', axis=0, tiled=...  74 us
    psum x1, blocking collectives, local(): lax.psum((sum_w1, sum_b1, sum_w2), ('face', 'sub'))  36.3 us
    psum x1, waiting for transfers between devices, local(): lax.psum((sum_w1, sum_b1, sum_w2), ('face', 'sub'))  23.3 us
    all_gather x2, blocking collectives, fetch_halo(): lax.all_gather(own_rows[None], 'face', axis=0, tiled=True)  17.3 us
    all_gather x2, blocking collectives, return_halo(): lax.all_gather(own_rows[None].astype(jnp.bfloat16), 'face', axis=0, tiled...  15.4 us
    add x14, other arithmetic, scatter_windows(): summed.at[row_off:row_off + extent, col_off:col_off + extent].add(portion)  14.4 us
  transfers between devices with their start and end apart: 1, of which 1 were waited for; matrix products, arithmetic and copies ran while one was open for 6% of the time, Pallas kernels for 0%

commit v1 on v0

v1 whole, which is shorter than its diff:
```python
import functools
import math

import jax
import jax.numpy as jnp
from jax import lax
from jax.experimental import pallas as pl
from jax.experimental.pallas import tpu as pltpu
from jax.sharding import PartitionSpec as P

W = 32
F32, BF16 = jnp.float32, jnp.bfloat16
MESH = pl.DeviceIdType.MESH


def iota(shape, dim):
    return lax.broadcasted_iota(jnp.int32, shape, dim)


def hot(mask):
    return jnp.where(mask, 1.0, 0.0).astype(BF16)


def dot(a, b, ca=1, cb=0):
    return lax.dot_general(a, b, (((ca,), (cb,)), ((), ())), preferred_element_type=F32)


def split(x):
    hi = x.astype(BF16)
    return hi, (x - hi.astype(F32)).astype(BF16)


def rim_pos(q, extent, pad):
    e, p = q // W, q % W + pad
    far = extent - 1 + 2 * pad
    pos = jnp.where(e == 0, p, jnp.where(e == 1, p * W + far, jnp.where(e == 2, far * W + p, p * W)))
    return jnp.where(q % W < extent, pos, -1)


def kernel(S, F, chunk, scale, nbr, rot, feat, cot, w1, b1, w2,
           pooled, gin, gw1, gb1, gw2,
           send_mat, recv_mat, pad_in, pad_act, gpad1, gpad2, cotp,
           win_in, win_act, gs1, gs2, hidden, second, pg, gact,
           ex_out, ex_in, wf, wb, w1in, red, accf, w2in, gath,
           ex_ss, ex_rs, w_ss, w_rs):
    T, C = feat.shape[0], feat.shape[2]
    H = T // 2
    face, sub = lax.axis_index("face"), lax.axis_index("sub")
    me = face * S + sub
    part = chunk * S
    M, MP = T * W, (T + 2) * W

    def peers(count, mine, body):
        def step(d, c):
            body(lax.rem(mine + d, count))
            return c
        lax.fori_loop(1, count, step, 0)

    barrier = pltpu.get_barrier_semaphore()
    peers(S, sub, lambda j: pl.semaphore_signal(barrier, inc=1, device_id=(face, j), device_id_type=MESH))
    peers(F, face, lambda f: pl.semaphore_signal(barrier, inc=1, device_id=(f, sub), device_id_type=MESH))

    p32 = iota((W, 4 * W), 0)
    c32 = iota((W, 4 * W), 1)

    def put_slot(k, hit, src, flip, edge):
        tgt = jnp.where(flip == 1, src * W + T - 1 - p32, src * W + p32)
        base = pl.multiple_of(k * W, W)
        send_mat[pl.ds(base, W), :] = hot((c32 == tgt) & (p32 < T) & (hit == 1))
        recv_mat[pl.ds(base, W), :] = hot((c32 == edge * W + p32) & (p32 < T) & (edge >= 0))

    def edge_code(tile, e):
        r = rot[tile * 4 + e]
        x = (e + 2) % 4
        src = lax.rem(x + r, 4)
        odd = x % 2
        flip = jnp.where(r == 2, 1, jnp.where(r == 1, odd, jnp.where(r == 3, 1 - odd, 0)))
        return nbr[tile * 4 + e] == me, src, flip

    def in_face(j, c):
        hit, src, flip, edge = jnp.int32(0), jnp.int32(0), jnp.int32(0), jnp.int32(-1)
        for e in range(4):
            h, s, f = edge_code(face * S + j, e)
            hit = jnp.where(h, 1, hit)
            src = jnp.where(h, s, src)
            flip = jnp.where(h, f, flip)
            edge = jnp.where(nbr[me * 4 + e] == face * S + j, e, edge)
        put_slot(j, hit, src, flip, edge)
        return c

    lax.fori_loop(0, S, in_face, 0)

    def cross(f, c):
        for e in range(4):
            h, s, fl = edge_code(f * S + sub, e)
            other = f != face
            hit = jnp.where(h & other, 1, 0)
            edge = jnp.where((nbr[me * 4 + e] == f * S + sub) & other, e, -1)
            put_slot(S + f * 4 + e, hit, s, fl, edge)
        return c

    lax.fori_loop(0, F, cross, 0)

    for ph in range(4):
        ex_in[ph, pl.ds(pl.multiple_of(sub * W, W), W), :] = jnp.zeros((W, C), BF16)
        ex_in[ph, pl.ds(pl.multiple_of((S + 4 * face) * W, W), 4 * W), :] = jnp.zeros((4 * W, C), BF16)

    def ex_sub(ph, j, s_in, r_idx):
        return pltpu.make_async_remote_copy(
            src_ref=ex_out.at[ph, pl.ds(pl.multiple_of(j * W, W), W), :],
            dst_ref=ex_in.at[ph, pl.ds(pl.multiple_of(s_in * W, W), W), :],
            send_sem=ex_ss.at[ph, j], recv_sem=ex_rs.at[ph, r_idx],
            device_id=(face, j), device_id_type=MESH)

    def ex_face(ph, f, f_in):
        return pltpu.make_async_remote_copy(
            src_ref=ex_out.at[ph, pl.ds(pl.multiple_of((S + 4 * f) * W, W), 4 * W), :],
            dst_ref=ex_in.at[ph, pl.ds(pl.multiple_of((S + 4 * f_in) * W, W), 4 * W), :],
            send_sem=ex_ss.at[ph, S + f], recv_sem=ex_rs.at[ph, S + f_in],
            device_id=(f, sub), device_id_type=MESH)

    def ex_start(ph, mat, rims):
        ex_out[ph] = dot(mat[...], rims).astype(BF16)
        peers(S, sub, lambda j: ex_sub(ph, j, sub, sub).start())
        peers(F, face, lambda f: ex_face(ph, f, face).start())

    def ex_wait(ph, mat):
        peers(S, sub, lambda j: ex_sub(ph, j, j, j).wait_recv())
        peers(F, face, lambda f: ex_face(ph, f, f).wait_recv())
        return dot(mat[...], ex_in[ph], 0, 0)

    def ex_drain(ph):
        peers(S, sub, lambda j: ex_sub(ph, j, sub, sub).wait_send())
        peers(F, face, lambda f: ex_face(ph, f, face).wait_send())

    own_rims = hot(iota((4 * W, M), 1) == rim_pos(iota((4 * W, M), 0), T, 0))
    pad_rims = hot(iota((4 * W, MP), 1) == rim_pos(iota((4 * W, MP), 0), T, 1))
    own_place = hot(iota((M, 4 * W), 0) == rim_pos(iota((M, 4 * W), 1), T, 0))
    pad_place = hot(iota((MP, 4 * W), 0) == rim_pos(iota((MP, 4 * W), 1), T, 1))

    def windows(src, dst, rows):
        for b in range(3):
            dst[b] = src[:, b:b + W, :].reshape(rows * W, C).astype(BF16)

    def add_halo(padded, halo):
        placed = dot(pad_place, halo.astype(BF16)).reshape(T + 2, W, C)
        padded[:, 0:W, :] = padded[:, 0:W, :] + placed

    def conv(win, wt, out, rows, back):
        half = rows // 2

        def step(i, c):
            acc = None
            for a in range(3):
                for b in range(3):
                    off = pl.multiple_of(i * half, 16) + a * W
                    x = win[b, pl.ds(pl.multiple_of(off, 16), half), :]
                    tap = (2 - a) * 3 + 2 - b if back else a * 3 + b
                    d = dot(x, wt[tap * C:(tap + 1) * C, :], 1, 1 if back else 0)
                    acc = d if acc is None else acc + d
            out[pl.ds(pl.multiple_of(i * half, 16), half), :] = acc
            return c

        lax.fori_loop(0, 2, step, 0)

    def weight_grad(k, win, gs):
        for a in range(3):
            g = gs[2, (2 - a) * W:(2 - a) * W + MP, :]
            for b in range(3):
                t = a * 3 + b
                v = dot(win[b], g, 0, 0)
                wf[k, t * C:(t + 1) * C, :] = v
                wb[k, t * C:(t + 1) * C, :] = v.astype(BF16)

    pad_in[...] = jnp.zeros(pad_in.shape, F32)
    pad_in[1:T + 1, 1:T + 1, :] = feat[...].astype(F32)
    flat_in = pad_in[1:T + 1, 1:W + 1, :].reshape(M, C)
    rims = dot(own_rims, flat_in.astype(BF16)).astype(BF16)
    pl.semaphore_wait(barrier, S + F - 2)
    ex_start(0, send_mat, rims)

    cotp[...] = jnp.zeros(cotp.shape, F32)
    cotp[:, 0:H, :] = cot[...].astype(F32)
    r_up, c_up = iota((M, H * 16), 0), iota((M, H * 16), 1)
    spread = hot((r_up // (2 * W)) * 16 + (r_up % W) // 2 == c_up)
    up = dot(spread, cotp[...].reshape(H * 16, C).astype(BF16)) * 0.25
    gpad2[...] = jnp.zeros(gpad2.shape, F32)
    gpad2[2:T + 2, 2:T + 2, :] = up.reshape(T, W, C)[:, 0:T, :]
    windows(gpad2, gs2, T + 4)
    conv(gs2, w2, pg, MP, True)
    rims = dot(pad_rims, pg[...].astype(BF16)).astype(BF16)
    ex_start(2, recv_mat, rims)
    gact[...] = pg[...].reshape(T + 2, W, C)[1:T + 1]
    pad_act[...] = jnp.zeros(pad_act.shape, F32)
    gpad1[...] = jnp.zeros(gpad1.shape, F32)

    add_halo(pad_in, ex_wait(0, recv_mat))
    windows(pad_in, win_in, T + 2)
    conv(win_in, w1, hidden, M, False)
    hid = hidden[...] + b1[...]
    sig = 1.0 / (1.0 + jnp.exp(-hid))
    act = (hid * sig).astype(BF16)
    rims = dot(own_rims, act).astype(BF16)
    ex_start(1, send_mat, rims)
    pad_act[1:T + 1, 1:T + 1, :] = act.astype(F32).reshape(T, W, C)[:, 0:T, :]

    def fold(middle, arrived):
        hi, lo = split(arrived)
        back = dot(own_place, hi) + dot(own_place, lo)
        return middle[:, 1:T + 1, :] + back.reshape(T, W, C)[:, 0:T, :]

    ga = fold(gact, ex_wait(2, send_mat)).astype(BF16).astype(F32)
    slope = (sig * (1.0 + hid * (1.0 - sig))).reshape(T, W, C)[:, 0:T, :]
    gh = (ga * slope).astype(BF16).astype(F32)
    gpad1[2:T + 2, 2:T + 2, :] = gh
    windows(gpad1, gs1, T + 4)
    conv(gs1, w1, pg, MP, True)
    rims = dot(pad_rims, pg[...].astype(BF16)).astype(BF16)
    ex_start(3, recv_mat, rims)

    rows = wf.shape[1]

    def face_copy(k, st, f, f_in):
        return pltpu.make_async_remote_copy(
            src_ref=wb.at[k, pl.ds(pl.multiple_of(f * part, 16), part), :],
            dst_ref=w1in.at[k, f_in],
            send_sem=w_ss.at[k, 0, f], recv_sem=w_rs.at[k, 0, f_in],
            device_id=(f, sub), device_id_type=MESH)

    def sub_copy(k, j, j_in):
        return pltpu.make_async_remote_copy(
            src_ref=red.at[k, pl.ds(pl.multiple_of(j * chunk, 16), chunk), :],
            dst_ref=w2in.at[k, j_in],
            send_sem=w_ss.at[k, 1, j], recv_sem=w_rs.at[k, 1, j_in],
            device_id=(face, j), device_id_type=MESH)

    def sub_gather(k, j, own):
        place = gath.at[k, pl.ds(pl.multiple_of(face * part + own * chunk, 16), chunk), :]
        return pltpu.make_async_remote_copy(
            src_ref=place, dst_ref=place,
            send_sem=w_ss.at[k, 2, j], recv_sem=w_rs.at[k, 2, own],
            device_id=(face, j), device_id_type=MESH)

    def face_gather(k, f, own):
        place = gath.at[k, pl.ds(pl.multiple_of(own * part, 16), part), :]
        return pltpu.make_async_remote_copy(
            src_ref=place, dst_ref=place,
            send_sem=w_ss.at[k, 3, f], recv_sem=w_rs.at[k, 3, own],
            device_id=(f, sub), device_id_type=MESH)

    def reduce_start(k):
        peers(F, face, lambda f: face_copy(k, 0, f, face).start())

    def reduce_sub(k):
        peers(F, face, lambda f: face_copy(k, 0, f, f).wait_recv())
        accf[k] = wf[k, pl.ds(pl.multiple_of(face * part, 16), part), :]

        def add(f):
            accf[k] = accf[k] + w1in[k, f].astype(F32)
        peers(F, face, add)
        red[k] = accf[k].astype(BF16)
        peers(S, sub, lambda j: sub_copy(k, j, sub).start())

    def reduce_end(k):
        peers(S, sub, lambda j: sub_copy(k, j, j).wait_recv())
        own = pl.ds(pl.multiple_of(sub * chunk, 16), chunk)

        def step(d, tot):
            return tot + w2in[k, lax.rem(sub + d, S)].astype(F32)
        tot = lax.fori_loop(1, S, step, accf[k, own, :])
        gath[k, pl.ds(pl.multiple_of(face * part + sub * chunk, 16), chunk), :] = (tot * scale).astype(BF16)
        peers(S, sub, lambda j: sub_gather(k, j, sub).start())

    def gather_face(k):
        peers(S, sub, lambda j: sub_gather(k, j, j).wait_recv())
        peers(F, face, lambda f: face_gather(k, f, face).start())

    def gather_end(k, out):
        peers(F, face, lambda f: face_gather(k, f, f).wait_recv())
        out[...] = gath[k, 0:9 * C, :].astype(F32)

    def drain(k):
        peers(F, face, lambda f: face_copy(k, 0, f, face).wait_send())
        peers(S, sub, lambda j: sub_copy(k, j, sub).wait_send())
        peers(S, sub, lambda j: sub_gather(k, j, sub).wait_send())
        peers(F, face, lambda f: face_gather(k, f, face).wait_send())

    for k in range(2):
        wf[k, 9 * C:rows, :] = jnp.zeros((rows - 9 * C, C), F32)
        wb[k, 9 * C:rows, :] = jnp.zeros((rows - 9 * C, C), BF16)
    weight_grad(0, win_in, gs1)
    bias = jnp.sum(jnp.sum(gh, axis=0), axis=0, keepdims=True)
    bias = jnp.where(iota((16, C), 0) == 0, bias, 0.0)
    wf[0, 9 * C:9 * C + 16, :] = bias
    wb[0, 9 * C:9 * C + 16, :] = bias.astype(BF16)
    reduce_start(0)

    add_halo(pad_act, ex_wait(1, recv_mat))
    windows(pad_act, win_act, T + 2)
    weight_grad(1, win_act, gs2)
    reduce_start(1)
    reduce_sub(0)
    conv(win_act, w2, second, M, False)
    reduce_sub(1)
    hi, lo = split(second[...] + pad_in[1:T + 1, 1:W + 1, :].reshape(M, C))
    r_dn, c_dn = iota((H * 16, M), 0), iota((H * 16, M), 1)
    mean = hot((c_dn // (2 * W)) * 16 + (c_dn % W) // 2 == r_dn)
    down = (dot(mean, hi) + dot(mean, lo)) * 0.25
    pooled[...] = down.reshape(H, 16, C)[:, 0:H, :].astype(BF16)
    gact[...] = pg[...].reshape(T + 2, W, C)[1:T + 1]
    total = fold(gact, ex_wait(3, send_mat)) + gpad2[2:T + 2, 2:T + 2, :]
    gin[...] = total.astype(BF16)

    reduce_end(0)
    reduce_end(1)
    gather_face(0)
    gather_face(1)
    gather_end(0, gw1)
    gb1[...] = gath[0, 9 * C:9 * C + 16, :].astype(F32)[0:8]
    gather_end(1, gw2)
    for ph in range(4):
        ex_drain(ph)
    for k in range(2):
        drain(k)


def local(S, F, features, w_first, b_first, w_second, neighbours, rotations, cotangent):
    T, C = features.shape[1], features.shape[2]
    H = T // 2
    D = neighbours.shape[0]
    chunk = -(-(9 * C + 16) // (16 * D)) * 16
    rows, part = chunk * D, chunk * S
    K = (S + 4 * F) * W
    scale = 1.0 / math.sqrt(D * T * T)
    vm = pl.BlockSpec(memory_space=pltpu.VMEM)
    sm = pl.BlockSpec(memory_space=pltpu.SMEM)
    n = max(S, F)
    pooled, gin, gw1, gb1, gw2 = pl.pallas_call(
        functools.partial(kernel, S, F, chunk, scale),
        out_shape=(
            jax.ShapeDtypeStruct((H, H, C), BF16),
            jax.ShapeDtypeStruct((T, T, C), BF16),
            jax.ShapeDtypeStruct((9 * C, C), F32),
            jax.ShapeDtypeStruct((8, C), F32),
            jax.ShapeDtypeStruct((9 * C, C), F32),
        ),
        in_specs=[sm, sm, vm, vm, vm, vm, vm],
        out_specs=(vm,) * 5,
        scratch_shapes=[
            pltpu.VMEM((K, 4 * W), BF16),
            pltpu.VMEM((K, 4 * W), BF16),
            pltpu.VMEM((T + 2, W + 8, C), F32),
            pltpu.VMEM((T + 2, W + 8, C), F32),
            pltpu.VMEM((T + 4, W + 8, C), F32),
            pltpu.VMEM((T + 4, W + 8, C), F32),
            pltpu.VMEM((H, 16, C), F32),
            pltpu.VMEM((3, (T + 2) * W, C), BF16),
            pltpu.VMEM((3, (T + 2) * W, C), BF16),
            pltpu.VMEM((3, (T + 4) * W, C), BF16),
            pltpu.VMEM((3, (T + 4) * W, C), BF16),
            pltpu.VMEM((T * W, C), F32),
            pltpu.VMEM((T * W, C), F32),
            pltpu.VMEM(((T + 2) * W, C), F32),
            pltpu.VMEM((T, W, C), F32),
            pltpu.VMEM((4, K, C), BF16),
            pltpu.VMEM((4, K, C), BF16),
            pltpu.VMEM((2, rows, C), F32),
            pltpu.VMEM((2, rows, C), BF16),
            pltpu.VMEM((2, F, part, C), BF16),
            pltpu.VMEM((2, part, C), BF16),
            pltpu.VMEM((2, part, C), F32),
            pltpu.VMEM((2, S, chunk, C), BF16),
            pltpu.VMEM((2, rows, C), BF16),
            pltpu.SemaphoreType.DMA((4, S + F)),
            pltpu.SemaphoreType.DMA((4, S + F)),
            pltpu.SemaphoreType.DMA((2, 4, n)),
            pltpu.SemaphoreType.DMA((2, 4, n)),
        ],
        compiler_params=pltpu.CompilerParams(
            collective_id=0, has_side_effects=True, vmem_limit_bytes=56 * 1024 * 1024
        ),
        name="level",
    )(
        neighbours.reshape(-1), rotations.reshape(-1), features, cotangent,
        w_first.reshape(9 * C, C), b_first.reshape(1, C), w_second.reshape(9 * C, C),
    )
    return (pooled, gin, gw1.reshape(3, 3, C, C), gb1[0], gw2.reshape(3, 3, C, C))


def solution(mesh):
    tiles = P(("face", "sub"), None, None)
    return jax.shard_map(
        functools.partial(local, mesh.shape["sub"], mesh.shape["face"]),
        mesh=mesh,
        in_specs=(tiles, P(), P(), P(), P(), P(), tiles),
        out_specs=(tiles, tiles, P(), P(), P()),
        check_vma=False,
    )
```

time: 463 us -> 97.7 us (0.21)
  the two profiles are of different devices: /device:TPU:1 before, /device:TPU:17 now
where the time goes in v1:
time: 97.7 us; the launch traced here: 97.4 us
  Pallas kernels  85.3 us (87%)
  local copies, waits for them, and re-layouts  11.4 us (12%)
    pallas_call x1, Pallas kernels, local(): pl.pallas_call(functools.partial(kernel, S, F, chunk, scale), out_shape=(...  85.3 us
    unnamed x8, local copies, waits for them, and re-layouts  8.89 us

profile of v1, /device:TPU:17, one launch (start us, length us, event | category | flops | bytes accessed | tf_op | source)
XLA Modules:
  0.0 97.4 jit_solution(11290344658688436460)
XLA Ops:
  0.6 0.8 copy.14
  1.4 0.6 reshape.31.nbr
  2.0 0.8 copy.15
  2.8 0.6 reshape.32.rot
  3.4 85.3 %level.1 = (bf16[12,12,192]{2,1,0:T(8,128)(2,1)}, bf16[24,24,192]{2,1,0:T(8,128)(2,1)}, f32[1728,192]{1,0:T(8,128)}, f32[8,192]{1,0:T(8,128)}, f32[1728,192]{1,0:T(8,128)}) custom-call(s32[128]{0:T(128)} %reshape.31.nbr, s32[128]{0:T(128)} %reshape.32.rot, bf16[24,24,192]{2,1,0:T(8,128)(2,1)} %feat.1, bf16[12,12,192]{2,1,0:T(8,128)(2,1)} %cot.1, ...), custom_call_target="tpu_custom_call" | custom-call | tf_op jit(solution)/shard_map/level/pallas_call | solution.py:338
  88.7 1.3 %slice.3 = f32[1,192]{1,0:T(1,128)} slice(f32[8,192]{1,0:T(8,128)} %get-tuple-element.13), slice={[0:1], [0:192]} | slice | bytes 1536 | tf_op jit(solution)/shard_map/slice | solution.py:387
  90.0 1.5 %copy.20 = bf16[12,12,192]{2,1,0:T(8,128)(2,1)} copy(bf16[12,12,192]{2,1,0:T(8,128)(2,1)} %get-tuple-element.20) | data formatting | bytes 110592
  91.5 1.7 %copy.21 = bf16[24,24,192]{2,1,0:T(8,128)(2,1)} copy(bf16[24,24,192]{2,1,0:T(8,128)(2,1)} %get-tuple-element.21) | data formatting | bytes 442368
  93.2 0.0 copy-start
  93.2 2.9 %copy.22 = f32[3,3,192,192]{3,2,1,0:T(8,128)} copy(f32[3,3,192,192]{3,2,1,0:T(8,128)} %bitcast.7) | data formatting | bytes 2654208
  96.1 0.0 copy-done
  96.1 1.2 %copy.23 = f32[3,3,192,192]{3,2,1,0:T(8,128)} copy(f32[3,3,192,192]{3,2,1,0:T(8,128)S(1)} %bitcast.6) | data formatting | bytes 2654208
Async XLA Ops:
  93.2 2.9 %copy-start = (f32[1728,192]{1,0:T(8,128)S(1)}, f32[1728,192]{1,0:T(8,128)}, u32[]{:S(2)}) copy-start(f32[1728,192]{1,0:T(8,128)} %get-tuple-element.14) | copy-start | bytes 3981316

commit v2 on v1

--- a/solution.py
+++ b/solution.py
@@ -8,6 +8,7 @@
 from jax.experimental.pallas import tpu as pltpu
 from jax.sharding import PartitionSpec as P
 
+LANES = 128
 W = 32
 F32, BF16 = jnp.float32, jnp.bfloat16
 MESH = pl.DeviceIdType.MESH
@@ -31,23 +32,31 @@
 
 
 def rim_pos(q, extent, pad):
-    e, p = q // W, q % W + pad
+    e, p = q >> 5, (q & (W - 1)) + pad
     far = extent - 1 + 2 * pad
     pos = jnp.where(e == 0, p, jnp.where(e == 1, p * W + far, jnp.where(e == 2, far * W + p, p * W)))
-    return jnp.where(q % W < extent, pos, -1)
+    return jnp.where((q & (W - 1)) < extent, pos, -1)
+
+
+def pool_pos(r):
+    return ((r >> 6) << 4) + ((r & (W - 1)) >> 1)
 
 
 def kernel(S, F, chunk, scale, nbr, rot, feat, cot, w1, b1, w2,
-           pooled, gin, gw1, gb1, gw2,
+           pooled, gin, gath,
            send_mat, recv_mat, pad_in, pad_act, gpad1, gpad2, cotp,
            win_in, win_act, gs1, gs2, hidden, second, pg, gact,
-           ex_out, ex_in, wf, wb, w1in, red, accf, w2in, gath,
+           ex_out, ex_in, wf, wb, w1in, red, accf, w2in, red2, acc2, w3in,
            ex_ss, ex_rs, w_ss, w_rs):
     T, C = feat.shape[0], feat.shape[2]
     H = T // 2
     face, sub = lax.axis_index("face"), lax.axis_index("sub")
     me = face * S + sub
     part = chunk * S
+    A = 4 if S % 4 == 0 else 1
+    B = S // A
+    a_id, b_id = sub // B, lax.rem(sub, B)
+    group = chunk * A
     M, MP = T * W, (T + 2) * W
 
     def peers(count, mine, body):
@@ -72,7 +81,7 @@
     def edge_code(tile, e):
         r = rot[tile * 4 + e]
         x = (e + 2) % 4
-        src = lax.rem(x + r, 4)
+        src = (x + r) & 3
         odd = x % 2
         flip = jnp.where(r == 2, 1, jnp.where(r == 1, odd, jnp.where(r == 3, 1 - odd, 0)))
         return nbr[tile * 4 + e] == me, src, flip
@@ -133,10 +142,10 @@
         peers(S, sub, lambda j: ex_sub(ph, j, sub, sub).wait_send())
         peers(F, face, lambda f: ex_face(ph, f, face).wait_send())
 
-    own_rims = hot(iota((4 * W, M), 1) == rim_pos(iota((4 * W, M), 0), T, 0))
-    pad_rims = hot(iota((4 * W, MP), 1) == rim_pos(iota((4 * W, MP), 0), T, 1))
-    own_place = hot(iota((M, 4 * W), 0) == rim_pos(iota((M, 4 * W), 1), T, 0))
-    pad_place = hot(iota((MP, 4 * W), 0) == rim_pos(iota((MP, 4 * W), 1), T, 1))
+    own_rims = hot(iota((4 * W, M), 1) == rim_pos(iota((4 * W, 1), 0), T, 0))
+    pad_rims = hot(iota((4 * W, MP), 1) == rim_pos(iota((4 * W, 1), 0), T, 1))
+    own_place = hot(iota((M, 4 * W), 0) == rim_pos(iota((1, 4 * W), 1), T, 0))
+    pad_place = hot(iota((MP, 4 * W), 0) == rim_pos(iota((1, 4 * W), 1), T, 1))
 
     def windows(src, dst, rows):
         for b in range(3):
@@ -163,14 +172,22 @@
 
         lax.fori_loop(0, 2, step, 0)
 
+    def put(k, r, v):
+        wf[k, r:r + v.shape[0], :] = v
+        wb[k, r:r + v.shape[0], :] = v.astype(BF16)
+
     def weight_grad(k, win, gs):
-        for a in range(3):
-            g = gs[2, (2 - a) * W:(2 - a) * W + MP, :]
-            for b in range(3):
-                t = a * 3 + b
-                v = dot(win[b], g, 0, 0)
-                wf[k, t * C:(t + 1) * C, :] = v
-                wb[k, t * C:(t + 1) * C, :] = v.astype(BF16)
+        odd = None
+        for t in range(9):
+            a, b = t // 3, t % 3
+            v = dot(win[b], gs[2, (2 - a) * W:(2 - a) * W + MP, :], 0, 0)
+            put(k, t * C, v[:, 0:LANES])
+            rest = v[:, LANES:C]
+            if t % 2 == 0:
+                odd = rest
+            if t % 2 == 1 or t == 8:
+                pair = jnp.concatenate([odd, rest], axis=1)
+                put(k, (9 + t // 2) * C, pair)
 
     pad_in[...] = jnp.zeros(pad_in.shape, F32)
     pad_in[1:T + 1, 1:T + 1, :] = feat[...].astype(F32)
@@ -181,8 +198,7 @@
 
     cotp[...] = jnp.zeros(cotp.shape, F32)
     cotp[:, 0:H, :] = cot[...].astype(F32)
-    r_up, c_up = iota((M, H * 16), 0), iota((M, H * 16), 1)
-    spread = hot((r_up // (2 * W)) * 16 + (r_up % W) // 2 == c_up)
+    spread = hot(pool_pos(iota((M, 1), 0)) == iota((M, H * 16), 1))
     up = dot(spread, cotp[...].reshape(H * 16, C).astype(BF16)) * 0.25
     gpad2[...] = jnp.zeros(gpad2.shape, F32)
     gpad2[2:T + 2, 2:T + 2, :] = up.reshape(T, W, C)[:, 0:T, :]
@@ -227,125 +243,174 @@
             send_sem=w_ss.at[k, 0, f], recv_sem=w_rs.at[k, 0, f_in],
             device_id=(f, sub), device_id_type=MESH)
 
-    def sub_copy(k, j, j_in):
-        return pltpu.make_async_remote_copy(
-            src_ref=red.at[k, pl.ds(pl.multiple_of(j * chunk, 16), chunk), :],
+    def b_copy(k, j, j_in):
+        return pltpu.make_async_remote_copy(
+            src_ref=red.at[k, pl.ds(pl.multiple_of(j * group, 16), group), :],
             dst_ref=w2in.at[k, j_in],
             send_sem=w_ss.at[k, 1, j], recv_sem=w_rs.at[k, 1, j_in],
-            device_id=(face, j), device_id_type=MESH)
-
-    def sub_gather(k, j, own):
-        place = gath.at[k, pl.ds(pl.multiple_of(face * part + own * chunk, 16), chunk), :]
+            device_id=(face, a_id * B + j), device_id_type=MESH)
+
+    def a_copy(k, j, j_in):
+        return pltpu.make_async_remote_copy(
+            src_ref=red2.at[k, pl.ds(pl.multiple_of(j * chunk, 16), chunk), :],
+            dst_ref=w3in.at[k, j_in],
+            send_sem=w_ss.at[k, 2, j], recv_sem=w_rs.at[k, 2, j_in],
+            device_id=(face, j * B + b_id), device_id_type=MESH)
+
+    def spot(k, start, size):
+        return gath.at[k, pl.ds(pl.multiple_of(start, 16), size), :]
+
+    def a_gather(k, j, own):
+        place = spot(k, face * part + b_id * group + own * chunk, chunk)
         return pltpu.make_async_remote_copy(
             src_ref=place, dst_ref=place,
-            send_sem=w_ss.at[k, 2, j], recv_sem=w_rs.at[k, 2, own],
-            device_id=(face, j), device_id_type=MESH)
+            send_sem=w_ss.at[k, 3, j], recv_sem=w_rs.at[k, 3, own],
+            device_id=(face, j * B + b_id), device_id_type=MESH)
+
+    def b_gather(k, j, own):
+        place = spot(k, face * part + own * group, group)
+        return pltpu.make_async_remote_copy(
+            src_ref=place, dst_ref=place,
+            send_sem=w_ss.at[k, 4, j], recv_sem=w_rs.at[k, 4, own],
+            device_id=(face, a_id * B + j), device_id_type=MESH)
 
     def face_gather(k, f, own):
-        place = gath.at[k, pl.ds(pl.multiple_of(own * part, 16), part), :]
+        place = spot(k, own * part, part)
         return pltpu.make_async_remote_copy(
             src_ref=place, dst_ref=place,
-            send_sem=w_ss.at[k, 3, f], recv_sem=w_rs.at[k, 3, own],
+            send_sem=w_ss.at[k, 5, f], recv_sem=w_rs.at[k, 5, own],
             device_id=(f, sub), device_id_type=MESH)
 
     def reduce_start(k):
         peers(F, face, lambda f: face_copy(k, 0, f, face).start())
 
-    def reduce_sub(k):
+    def summed(first, count, mine, ref, k):
+        def step(d, tot):
+            return tot + ref[k, lax.rem(mine + d, count)].astype(F32)
+        return lax.fori_loop(1, count, step, first)
+
+    def reduce_b(k):
         peers(F, face, lambda f: face_copy(k, 0, f, f).wait_recv())
-        accf[k] = wf[k, pl.ds(pl.multiple_of(face * part, 16), part), :]
-
-        def add(f):
-            accf[k] = accf[k] + w1in[k, f].astype(F32)
-        peers(F, face, add)
-        red[k] = accf[k].astype(BF16)
-        peers(S, sub, lambda j: sub_copy(k, j, sub).start())
-
-    def reduce_end(k):
-        peers(S, sub, lambda j: sub_copy(k, j, j).wait_recv())
-        own = pl.ds(pl.multiple_of(sub * chunk, 16), chunk)
-
-        def step(d, tot):
-            return tot + w2in[k, lax.rem(sub + d, S)].astype(F32)
-        tot = lax.fori_loop(1, S, step, accf[k, own, :])
-        gath[k, pl.ds(pl.multiple_of(face * part + sub * chunk, 16), chunk), :] = (tot * scale).astype(BF16)
-        peers(S, sub, lambda j: sub_gather(k, j, sub).start())
+        for r in range(B):
+            at = pl.ds(pl.multiple_of(face * part + r * group, 16), group)
+            tot = wf[k, at, :]
+            for f in range(1, F):
+                tot = tot + w1in[k, lax.rem(face + f, F), r * group:(r + 1) * group, :].astype(F32)
+            accf[k, r * group:(r + 1) * group, :] = tot
+            red[k, r * group:(r + 1) * group, :] = tot.astype(BF16)
+        peers(B, b_id, lambda j: b_copy(k, j, b_id).start())
+
+    def reduce_a(k):
+        peers(B, b_id, lambda j: b_copy(k, j, j).wait_recv())
+        tot = summed(accf[k, pl.ds(pl.multiple_of(b_id * group, 16), group), :], B, b_id, w2in, k)
+        acc2[k] = tot
+        red2[k] = tot.astype(BF16)
+        peers(A, a_id, lambda j: a_copy(k, j, a_id).start())
+
+    def gather_a(k):
+        peers(A, a_id, lambda j: a_copy(k, j, j).wait_recv())
+        tot = summed(acc2[k, pl.ds(pl.multiple_of(a_id * chunk, 16), chunk), :], A, a_id, w3in, k)
+        own = pl.ds(pl.multiple_of(face * part + b_id * group + a_id * chunk, 16), chunk)
+        gath[k, own, :] = (tot * scale).astype(BF16)
+        peers(A, a_id, lambda j: a_gather(k, j, a_id).start())
+
+    def gather_b(k):
+        peers(A, a_id, lambda j: a_gather(k, j, j).wait_recv())
+        peers(B, b_id, lambda j: b_gather(k, j, b_id).start())
 
     def gather_face(k):
-        peers(S, sub, lambda j: sub_gather(k, j, j).wait_recv())
+        peers(B, b_id, lambda j: b_gather(k, j, j).wait_recv())
         peers(F, face, lambda f: face_gather(k, f, face).start())
 
-    def gather_end(k, out):
+    def gather_end(k):
         peers(F, face, lambda f: face_gather(k, f, f).wait_recv())
-        out[...] = gath[k, 0:9 * C, :].astype(F32)
 
     def drain(k):
         peers(F, face, lambda f: face_copy(k, 0, f, face).wait_send())
-        peers(S, sub, lambda j: sub_copy(k, j, sub).wait_send())
-        peers(S, sub, lambda j: sub_gather(k, j, sub).wait_send())
+        peers(B, b_id, lambda j: b_copy(k, j, b_id).wait_send())
+        peers(A, a_id, lambda j: a_copy(k, j, a_id).wait_send())
+        peers(A, a_id, lambda j: a_gather(k, j, a_id).wait_send())
+        peers(B, b_id, lambda j: b_gather(k, j, b_id).wait_send())
         peers(F, face, lambda f: face_gather(k, f, face).wait_send())
 
     for k in range(2):
-        wf[k, 9 * C:rows, :] = jnp.zeros((rows - 9 * C, C), F32)
-        wb[k, 9 * C:rows, :] = jnp.zeros((rows - 9 * C, C), BF16)
+        put(k, 14 * C, jnp.zeros((rows - 14 * C, LANES), F32))
     weight_grad(0, win_in, gs1)
     bias = jnp.sum(jnp.sum(gh, axis=0), axis=0, keepdims=True)
-    bias = jnp.where(iota((16, C), 0) == 0, bias, 0.0)
-    wf[0, 9 * C:9 * C + 16, :] = bias
-    wb[0, 9 * C:9 * C + 16, :] = bias.astype(BF16)
+    bias = jnp.concatenate([bias, jnp.zeros((1, 2 * LANES - C), F32)], axis=1)
+    line = iota((16, LANES), 0)
+    put(0, 14 * C, jnp.where(line == 0, bias[:, 0:LANES], jnp.where(line == 1, bias[:, LANES:], 0.0)))
     reduce_start(0)
 
     add_halo(pad_act, ex_wait(1, recv_mat))
     windows(pad_act, win_act, T + 2)
+    reduce_b(0)
     weight_grad(1, win_act, gs2)
     reduce_start(1)
-    reduce_sub(0)
+    reduce_a(0)
     conv(win_act, w2, second, M, False)
-    reduce_sub(1)
+    reduce_b(1)
+    gather_a(0)
     hi, lo = split(second[...] + pad_in[1:T + 1, 1:W + 1, :].reshape(M, C))
-    r_dn, c_dn = iota((H * 16, M), 0), iota((H * 16, M), 1)
-    mean = hot((c_dn // (2 * W)) * 16 + (c_dn % W) // 2 == r_dn)
+    mean = hot(pool_pos(iota((1, M), 1)) == iota((H * 16, M), 0))
     down = (dot(mean, hi) + dot(mean, lo)) * 0.25
     pooled[...] = down.reshape(H, 16, C)[:, 0:H, :].astype(BF16)
     gact[...] = pg[...].reshape(T + 2, W, C)[1:T + 1]
     total = fold(gact, ex_wait(3, send_mat)) + gpad2[2:T + 2, 2:T + 2, :]
     gin[...] = total.astype(BF16)
 
-    reduce_end(0)
-    reduce_end(1)
+    gather_b(0)
+    reduce_a(1)
+    gather_a(1)
     gather_face(0)
+    gather_b(1)
+    gather_end(0)
     gather_face(1)
-    gather_end(0, gw1)
-    gb1[...] = gath[0, 9 * C:9 * C + 16, :].astype(F32)[0:8]
-    gather_end(1, gw2)
+    gather_end(1)
     for ph in range(4):
         ex_drain(ph)
     for k in range(2):
         drain(k)
 
 
+def finish(C, pooled_in, gin_in, gath, pooled, gin, gw1, gb1, gw2):
+    pooled[...] = pooled_in[...]
+    gin[...] = gin_in[...]
+    for k, out in ((0, gw1), (1, gw2)):
+        for t in range(9):
+            left = gath[k, t * C:(t + 1) * C, :].astype(F32)
+            pair = gath[k, (9 + t // 2) * C:(10 + t // 2) * C, :].astype(F32)
+            half = C - LANES
+            right = pair[:, 0:half] if t % 2 == 0 else pair[:, half:2 * half]
+            out[t // 3, t % 3, :, 0:LANES] = left
+            out[t // 3, t % 3, :, LANES:C] = right
+    bias = gath[0, 14 * C:14 * C + 16, :].astype(F32)
+    gb1[:, 0:LANES] = bias[0:1]
+    gb1[:, LANES:C] = bias[1:2, 0:C - LANES]
+
+
 def local(S, F, features, w_first, b_first, w_second, neighbours, rotations, cotangent):
     T, C = features.shape[1], features.shape[2]
     H = T // 2
     D = neighbours.shape[0]
-    chunk = -(-(9 * C + 16) // (16 * D)) * 16
+    chunk = -(-(14 * C + 16) // (16 * D)) * 16
+    A = 4 if S % 4 == 0 else 1
+    B = S // A
     rows, part = chunk * D, chunk * S
     K = (S + 4 * F) * W
     scale = 1.0 / math.sqrt(D * T * T)
     vm = pl.BlockSpec(memory_space=pltpu.VMEM)
     sm = pl.BlockSpec(memory_space=pltpu.SMEM)
     n = max(S, F)
-    pooled, gin, gw1, gb1, gw2 = pl.pallas_call(
+    pooled, gin, gath = pl.pallas_call(
         functools.partial(kernel, S, F, chunk, scale),
         out_shape=(
             jax.ShapeDtypeStruct((H, H, C), BF16),
             jax.ShapeDtypeStruct((T, T, C), BF16),
-            jax.ShapeDtypeStruct((9 * C, C), F32),
-            jax.ShapeDtypeStruct((8, C), F32),
-            jax.ShapeDtypeStruct((9 * C, C), F32),
+            jax.ShapeDtypeStruct((2, rows, LANES), BF16),
         ),
         in_specs=[sm, sm, vm, vm, vm, vm, vm],
-        out_specs=(vm,) * 5,
+        out_specs=(vm,) * 3,
         scratch_shapes=[
             pltpu.VMEM((K, 4 * W), BF16),
             pltpu.VMEM((K, 4 * W), BF16),
@@ -364,17 +429,19 @@
             pltpu.VMEM((T, W, C), F32),
             pltpu.VMEM((4, K, C), BF16),
             pltpu.VMEM((4, K, C), BF16),
-            pltpu.VMEM((2, rows, C), F32),
-            pltpu.VMEM((2, rows, C), BF16),
-            pltpu.VMEM((2, F, part, C), BF16),
-            pltpu.VMEM((2, part, C), BF16),
-            pltpu.VMEM((2, part, C), F32),
-            pltpu.VMEM((2, S, chunk, C), BF16),
-            pltpu.VMEM((2, rows, C), BF16),
+            pltpu.VMEM((2, rows, LANES), F32),
+            pltpu.VMEM((2, rows, LANES), BF16),
+            pltpu.VMEM((2, F, part, LANES), BF16),
+            pltpu.VMEM((2, part, LANES), BF16),
+            pltpu.VMEM((2, part, LANES), F32),
+            pltpu.VMEM((2, B, A * chunk, LANES), BF16),
+            pltpu.VMEM((2, A * chunk, LANES), BF16),
+            pltpu.VMEM((2, A * chunk, LANES), F32),
+            pltpu.VMEM((2, A, chunk, LANES), BF16),
             pltpu.SemaphoreType.DMA((4, S + F)),
             pltpu.SemaphoreType.DMA((4, S + F)),
-            pltpu.SemaphoreType.DMA((2, 4, n)),
-            pltpu.SemaphoreType.DMA((2, 4, n)),
+            pltpu.SemaphoreType.DMA((2, 6, n)),
+            pltpu.SemaphoreType.DMA((2, 6, n)),
         ],
         compiler_params=pltpu.CompilerParams(
             collective_id=0, has_side_effects=True, vmem_limit_bytes=56 * 1024 * 1024
@@ -384,7 +451,21 @@
         neighbours.reshape(-1), rotations.reshape(-1), features, cotangent,
         w_first.reshape(9 * C, C), b_first.reshape(1, C), w_second.reshape(9 * C, C),
     )
-    return (pooled, gin, gw1.reshape(3, 3, C, C), gb1[0], gw2.reshape(3, 3, C, C))
+    pooled, gin, gw1, gb1, gw2 = pl.pallas_call(
+        functools.partial(finish, C),
+        out_shape=(
+            jax.ShapeDtypeStruct((H, H, C), BF16),
+            jax.ShapeDtypeStruct((T, T, C), BF16),
+            jax.ShapeDtypeStruct((3, 3, C, C), F32),
+            jax.ShapeDtypeStruct((1, C), F32),
+            jax.ShapeDtypeStruct((3, 3, C, C), F32),
+        ),
+        in_specs=[vm] * 3,
+        out_specs=(vm,) * 5,
+        compiler_params=pltpu.CompilerParams(vmem_limit_bytes=24 * 1024 * 1024),
+        name="finish",
+    )(pooled, gin, gath)
+    return (pooled, gin, gw1, gb1.reshape(C), gw2)
 
 
 def solution(mesh):

time: 97.7 us -> 76.6 us (0.78)
  the two profiles are of different devices: /device:TPU:17 before, /device:TPU:1 now
where the time goes in v2:
time: 76.6 us; the launch traced here: 76.3 us
  Pallas kernels  69.6 us (91%)
  local copies, waits for them, and re-layouts  6.02 us (8%)
    pallas_call x1, Pallas kernels, local(): pl.pallas_call(functools.partial(kernel, S, F, chunk, scale), out_shape=(...  67.6 us
    unnamed x8, local copies, waits for them, and re-layouts  4.78 us
    pallas_call x1, Pallas kernels, local(): pl.pallas_call(functools.partial(finish, C), out_shape=(jax.ShapeDtypeStr...  2.04 us

profile of v2, /device:TPU:1, one launch (start us, length us, event | category | flops | bytes accessed | tf_op | source)
XLA Modules:
  0.0 76.3 jit_solution(3259851246711251174)
XLA Ops:
  0.6 0.8 %copy.14 = s32[32,4]{1,0:T(8,128)S(1)} copy(s32[32,4]{0,1:T(4,128)} %param.11) | data formatting | bytes 1024 | tf_op args[4]
  1.4 0.6 reshape.28.nbr
  2.0 0.8 copy.15
  2.8 0.6 reshape.29.rot
  3.4 67.6 %level.1 = (bf16[12,12,192]{2,1,0:T(8,128)(2,1)}, bf16[24,24,192]{2,1,0:T(8,128)(2,1)}, bf16[2,3072,128]{2,1,0:T(8,128)(2,1)}) custom-call(s32[128]{0:T(128)} %reshape.28.nbr, s32[128]{0:T(128)} %reshape.29.rot, bf16[24,24,192]{2,1,0:T(8,128)(2,1)} %feat.1, bf16[12,12,192]{2,1,0:T(8,128)(2,1)} %cot.1, bf16[1728,192]{1,0:T(8,128)(2,1)} %bitcast.4, ...), custom_call_target="tpu_custom_call" | custom-call | tf_op jit(solution)/shard_map/level/pallas_call | solution.py:405
  71.0 0.0 copy-start
  71.0 1.4 %copy-done = bf16[2,3072,128]{2,1,0:T(8,128)(2,1)S(1)} copy-done((bf16[2,3072,128]{2,1,0:T(8,128)(2,1)S(1)}, bf16[2,3072,128]{2,1,0:T(8,128)(2,1)}, u32[]{:S(2)}) %copy-start) | copy-done | bytes 1572888
  72.4 0.0 copy-start.1
  72.4 1.0 %copy-done.1 = bf16[24,24,192]{2,1,0:T(8,128)(2,1)S(1)} copy-done((bf16[24,24,192]{2,1,0:T(8,128)(2,1)S(1)}, bf16[24,24,192]{2,1,0:T(8,128)(2,1)}, u32[]{:S(2)}) %copy-start.1) | copy-done | bytes 221208
  73.4 0.0 copy-start.2
  73.4 0.9 %copy-done.2 = bf16[12,12,192]{2,1,0:T(8,128)(2,1)S(1)} copy-done((bf16[12,12,192]{2,1,0:T(8,128)(2,1)S(1)}, bf16[12,12,192]{2,1,0:T(8,128)(2,1)}, u32[]{:S(2)}) %copy-start.2) | copy-done | bytes 55320
  74.2 2.0 %finish.1 = (bf16[12,12,192]{2,1,0:T(8,128)(2,1)}, bf16[24,24,192]{2,1,0:T(8,128)(2,1)}, f32[3,3,192,192]{3,2,1,0:T(8,128)}, f32[1,192]{1,0:T(1,128)}, f32[3,3,192,192]{3,2,1,0:T(8,128)}) custom-call(bf16[12,12,192]{2,1,0:T(8,128)(2,1)S(1)} %copy-done.2, bf16[24,24,192]{2,1,0:T(8,128)(2,1)S(1)} %copy-done.1, bf16[2,3072,128]{2,1,0:T(8,128)(2,1)S(1)} %copy-done), custom_call_target="tpu_custom_call" | custom-call | tf_op jit(solution)/shard_map/finish/pallas_call | solution.py:454
Async XLA Ops:
  71.0 1.4 %copy-start = (bf16[2,3072,128]{2,1,0:T(8,128)(2,1)S(1)}, bf16[2,3072,128]{2,1,0:T(8,128)(2,1)}, u32[]{:S(2)}) copy-start(bf16[2,3072,128]{2,1,0:T(8,128)(2,1)} %get-tuple-element.15.gath) | copy-start | bytes 4718596
  72.4 1.0 %copy-start.1 = (bf16[24,24,192]{2,1,0:T(8,128)(2,1)S(1)}, bf16[24,24,192]{2,1,0:T(8,128)(2,1)}, u32[]{:S(2)}) copy-start(bf16[24,24,192]{2,1,0:T(8,128)(2,1)} %get-tuple-element.14.gin_in) | copy-start | bytes 663556
  73.4 0.9 %copy-start.2 = (bf16[12,12,192]{2,1,0:T(8,128)(2,1)S(1)}, bf16[12,12,192]{2,1,0:T(8,128)(2,1)}, u32[]{:S(2)}) copy-start(bf16[12,12,192]{2,1,0:T(8,128)(2,1)} %get-tuple-element.13.pooled_in) | copy-start | bytes 165892

commit v3 on v2

--- a/solution.py
+++ b/solution.py
@@ -79,12 +79,12 @@
         recv_mat[pl.ds(base, W), :] = hot((c32 == edge * W + p32) & (p32 < T) & (edge >= 0))
 
     def edge_code(tile, e):
-        r = rot[tile * 4 + e]
+        r = rot[tile, e]
         x = (e + 2) % 4
         src = (x + r) & 3
         odd = x % 2
         flip = jnp.where(r == 2, 1, jnp.where(r == 1, odd, jnp.where(r == 3, 1 - odd, 0)))
-        return nbr[tile * 4 + e] == me, src, flip
+        return nbr[tile, e] == me, src, flip
 
     def in_face(j, c):
         hit, src, flip, edge = jnp.int32(0), jnp.int32(0), jnp.int32(0), jnp.int32(-1)
@@ -93,7 +93,7 @@
             hit = jnp.where(h, 1, hit)
             src = jnp.where(h, s, src)
             flip = jnp.where(h, f, flip)
-            edge = jnp.where(nbr[me * 4 + e] == face * S + j, e, edge)
+            edge = jnp.where(nbr[me, e] == face * S + j, e, edge)
         put_slot(j, hit, src, flip, edge)
         return c
 
@@ -104,7 +104,7 @@
             h, s, fl = edge_code(f * S + sub, e)
             other = f != face
             hit = jnp.where(h & other, 1, 0)
-            edge = jnp.where((nbr[me * 4 + e] == f * S + sub) & other, e, -1)
+            edge = jnp.where((nbr[me, e] == f * S + sub) & other, e, -1)
             put_slot(S + f * 4 + e, hit, s, fl, edge)
         return c
 
@@ -156,7 +156,7 @@
         padded[:, 0:W, :] = padded[:, 0:W, :] + placed
 
     def conv(win, wt, out, rows, back):
-        half = rows // 2
+        half = rows
 
         def step(i, c):
             acc = None
@@ -170,7 +170,7 @@
             out[pl.ds(pl.multiple_of(i * half, 16), half), :] = acc
             return c
 
-        lax.fori_loop(0, 2, step, 0)
+        lax.fori_loop(0, 1, step, 0)
 
     def put(k, r, v):
         wf[k, r:r + v.shape[0], :] = v
@@ -230,9 +230,6 @@
     gh = (ga * slope).astype(BF16).astype(F32)
     gpad1[2:T + 2, 2:T + 2, :] = gh
     windows(gpad1, gs1, T + 4)
-    conv(gs1, w1, pg, MP, True)
-    rims = dot(pad_rims, pg[...].astype(BF16)).astype(BF16)
-    ex_start(3, recv_mat, rims)
 
     rows = wf.shape[1]
 
@@ -347,20 +344,22 @@
     reduce_b(0)
     weight_grad(1, win_act, gs2)
     reduce_start(1)
+    conv(gs1, w1, pg, MP, True)
+    rims = dot(pad_rims, pg[...].astype(BF16)).astype(BF16)
+    ex_start(3, recv_mat, rims)
     reduce_a(0)
+    reduce_b(1)
     conv(win_act, w2, second, M, False)
-    reduce_b(1)
     gather_a(0)
     hi, lo = split(second[...] + pad_in[1:T + 1, 1:W + 1, :].reshape(M, C))
     mean = hot(pool_pos(iota((1, M), 1)) == iota((H * 16, M), 0))
     down = (dot(mean, hi) + dot(mean, lo)) * 0.25
     pooled[...] = down.reshape(H, 16, C)[:, 0:H, :].astype(BF16)
+    reduce_a(1)
+    gather_b(0)
     gact[...] = pg[...].reshape(T + 2, W, C)[1:T + 1]
     total = fold(gact, ex_wait(3, send_mat)) + gpad2[2:T + 2, 2:T + 2, :]
     gin[...] = total.astype(BF16)
-
-    gather_b(0)
-    reduce_a(1)
     gather_a(1)
     gather_face(0)
     gather_b(1)
@@ -448,7 +447,7 @@
         ),
         name="level",
     )(
-        neighbours.reshape(-1), rotations.reshape(-1), features, cotangent,
+        neighbours, rotations, features, cotangent,
         w_first.reshape(9 * C, C), b_first.reshape(1, C), w_second.reshape(9 * C, C),
     )
     pooled, gin, gw1, gb1, gw2 = pl.pallas_call(

time: 76.6 us -> 74 us (0.966)
  Pallas kernels: 69.6 us -> 67 us
    pallas_call x1, Pallas kernels: 67.6 us -> 65 us  [local(): pl.pallas_call(functools.partial(kernel, S, F, chunk, scale), out_shape=(...]
    reshape x2 -> x0, local copies, waits for them, and re-layouts: 1.24 us -> none  [the longest x1 0.62 us: local(): neighbours.reshape(-1)]
    unnamed x8, local copies, waits for them, and re-layouts: 4.78 us -> 5.99 us
where the time goes in v3:
time: 74 us; the launch traced here: 73.7 us
  Pallas kernels  67 us (91%)
  local copies, waits for them, and re-layouts  5.99 us (8%)
    pallas_call x1, Pallas kernels, local(): pl.pallas_call(functools.partial(kernel, S, F, chunk, scale), out_shape=(...  65 us
    unnamed x8, local copies, waits for them, and re-layouts  5.99 us
    pallas_call x1, Pallas kernels, local(): pl.pallas_call(functools.partial(finish, C), out_shape=(jax.ShapeDtypeStr...  2.04 us

profile of v3, /device:TPU:1, one launch (start us, length us, event | category | flops | bytes accessed | tf_op | source)
XLA Modules:
  0.0 73.7 jit_solution(9284528696558696674)
XLA Ops:
  0.6 1.4 %copy.12.nbr = s32[32,4]{1,0:T(8,128)} copy(s32[32,4]{0,1:T(4,128)} %param.11) | data formatting | bytes 1024 | tf_op args[4]
  2.0 1.4 %copy.13.rot = s32[32,4]{1,0:T(8,128)} copy(s32[32,4]{0,1:T(4,128)} %param.12) | data formatting | bytes 1024 | tf_op args[5]
  3.4 65.0 %level.1 = (bf16[12,12,192]{2,1,0:T(8,128)(2,1)}, bf16[24,24,192]{2,1,0:T(8,128)(2,1)}, bf16[2,3072,128]{2,1,0:T(8,128)(2,1)}) custom-call(s32[32,4]{1,0:T(8,128)} %copy.12.nbr, s32[32,4]{1,0:T(8,128)} %copy.13.rot, bf16[24,24,192]{2,1,0:T(8,128)(2,1)} %feat.1, bf16[12,12,192]{2,1,0:T(8,128)(2,1)} %cot.1, bf16[1728,192]{1,0:T(8,128)(2,1)} %bitcast.4, ...), custom_call_target="tpu_custom_call" | custom-call | tf_op jit(solution)/shard_map/level/pallas_call | solution.py:404
  68.4 0.0 copy-start
  68.4 1.4 %copy-done = bf16[2,3072,128]{2,1,0:T(8,128)(2,1)S(1)} copy-done((bf16[2,3072,128]{2,1,0:T(8,128)(2,1)S(1)}, bf16[2,3072,128]{2,1,0:T(8,128)(2,1)}, u32[]{:S(2)}) %copy-start) | copy-done | bytes 1572888
  69.8 0.0 copy-start.1
  69.8 1.0 %copy-done.1 = bf16[24,24,192]{2,1,0:T(8,128)(2,1)S(1)} copy-done((bf16[24,24,192]{2,1,0:T(8,128)(2,1)S(1)}, bf16[24,24,192]{2,1,0:T(8,128)(2,1)}, u32[]{:S(2)}) %copy-start.1) | copy-done | bytes 221208
  70.7 0.0 copy-start.2
  70.7 0.9 %copy-done.2 = bf16[12,12,192]{2,1,0:T(8,128)(2,1)S(1)} copy-done((bf16[12,12,192]{2,1,0:T(8,128)(2,1)S(1)}, bf16[12,12,192]{2,1,0:T(8,128)(2,1)}, u32[]{:S(2)}) %copy-start.2) | copy-done | bytes 55320
  71.6 2.0 %finish.1 = (bf16[12,12,192]{2,1,0:T(8,128)(2,1)}, bf16[24,24,192]{2,1,0:T(8,128)(2,1)}, f32[3,3,192,192]{3,2,1,0:T(8,128)}, f32[1,192]{1,0:T(1,128)}, f32[3,3,192,192]{3,2,1,0:T(8,128)}) custom-call(bf16[12,12,192]{2,1,0:T(8,128)(2,1)S(1)} %copy-done.2, bf16[24,24,192]{2,1,0:T(8,128)(2,1)S(1)} %copy-done.1, bf16[2,3072,128]{2,1,0:T(8,128)(2,1)S(1)} %copy-done), custom_call_target="tpu_custom_call" | custom-call | tf_op jit(solution)/shard_map/finish/pallas_call | solution.py:453
Async XLA Ops:
  68.4 1.4 %copy-start = (bf16[2,3072,128]{2,1,0:T(8,128)(2,1)S(1)}, bf16[2,3072,128]{2,1,0:T(8,128)(2,1)}, u32[]{:S(2)}) copy-start(bf16[2,3072,128]{2,1,0:T(8,128)(2,1)} %get-tuple-element.15.gath) | copy-start | bytes 4718596
  69.8 1.0 %copy-start.1 = (bf16[24,24,192]{2,1,0:T(8,128)(2,1)S(1)}, bf16[24,24,192]{2,1,0:T(8,128)(2,1)}, u32[]{:S(2)}) copy-start(bf16[24,24,192]{2,1,0:T(8,128)(2,1)} %get-tuple-element.14.gin_in) | copy-start | bytes 663556
  70.7 0.9 %copy-start.2 = (bf16[12,12,192]{2,1,0:T(8,128)(2,1)S(1)}, bf16[12,12,192]{2,1,0:T(8,128)(2,1)}, u32[]{:S(2)}) copy-start(bf16[12,12,192]{2,1,0:T(8,128)(2,1)} %get-tuple-element.13.pooled_in) | copy-start | bytes 165892
